TPU v7x, 128 devices: a whole 4x4x4 slice. The times are simulated.
128 devices in a mesh: tm: 64 (over x, y, z), blk: 2 (over core).
Axes of the slice: x: 4, y: 4, z: 4, core: 2. Of those that a mesh axis runs over, the one named last changes fastest.
Arguments:
- initial_state: float32 [2, 1024], P(None, 'blk'), may hold values from -6 to 6
- decay_rate: float32 [1024], P('blk'), may hold values from 9.765625e-06 to 0.05
- step_sizes: float32 [2, 1024], P(None, 'tm'), may hold values from 0.5 to 514
- increments: float32 [2, 1024, 16], P(None, 'tm'), may hold values from -6 to 6
- coupling: float32 [16, 8, 128, 128], P(None, 'blk'), may hold values from -0.013671875 to 0.013671875
- input_weight: float32 [16, 1024], P(None, 'blk'), may hold values from -0.125 to 0.125
- gain: float32 [1024], P('blk'), may hold values from 0.1 to 1.9
- value_weight: bfloat16 [1024, 1024], P(None, 'blk'), may hold values from -0.1875 to 0.1875
- gate_weight: bfloat16 [1024, 1024], P(None, 'blk'), may hold values from -0.1875 to 0.1875
Outputs:
- states: float32 [2, 1024, 1024], P(None, 'tm', 'blk')
- readout: bfloat16 [2, 1024, 1024], P(None, 'tm', 'blk')
All inputs are finite; a program needn't handle non-finite values.
Results may differ from a plain program's by a relative error of at most 0.0051.
Values may be sent and summed in bfloat16 or wider, within the bound.
A program may use at most 128 MiB of HBM per device.

v0:
```python
import functools

import jax
import jax.numpy as jnp
from jax import lax
from jax.experimental import pallas as pl
from jax.experimental.pallas import tpu as pltpu
from jax.sharding import PartitionSpec as P

MESH = pl.DeviceIdType.MESH
F32, BF16 = jnp.float32, jnp.bfloat16
UNITS = 1024
L = 128
ROWS = 144
NODES = 48


def iota(shape, dim):
    return lax.broadcasted_iota(jnp.int32, shape, dim)


def split2(x):
    hi = x.astype(BF16)
    return hi, (x - hi.astype(F32)).astype(BF16)


def split3(x):
    hi = x.astype(BF16)
    rest = x - hi.astype(F32)
    mid = rest.astype(BF16)
    return hi, mid, (rest - mid.astype(F32)).astype(BF16)


def mm(a, b):
    return jnp.dot(a, b, preferred_element_type=F32)


def exact_mask_sum(mask, value):
    total = None
    for piece in split3(value):
        part = mm(mask, piece)
        total = part if total is None else total + part
    return total


def to_column(row):
    eye = iota((L, L), 0) == iota((L, L), 1)
    col = jnp.sum(jnp.where(eye, jnp.broadcast_to(row, (L, L)), 0.0), axis=1, keepdims=True)
    return jnp.broadcast_to(col, (L, L))


def kernel(
    h0_ref, decay_ref, steps_ref, inc_ref, coup_ref, iw_ref, gain_ref, vw_ref, gw_ref,
    states_ref, read_ref,
    pack, incbuf, cbuf, vw, gw, gbuf, cth, ctl, xbuf, dc, sig, arow, prow, ns, na,
    dbuf, eb, tree, pref, msg, maps, stout, stbuf,
    local_sem, inc_ss, inc_rs, gain_ss, gain_rs, map_ss, map_rs, st_ss, st_rs,
):
    tm, blk = lax.axis_index("tm"), lax.axis_index("blk")
    seg, chain = tm // 8, lax.rem(tm, 8)
    rec, lb = chain // 4, lax.rem(chain, 4)

    def peer(s, k, c):
        return (s * 8 + k, c)

    barrier = pltpu.get_barrier_semaphore()
    for i in range(1, 8):
        pl.semaphore_signal(barrier, inc=1, device_id=peer(seg, lax.rem(chain + i, 8), blk), device_id_type=MESH)
        pl.semaphore_signal(barrier, inc=1, device_id=peer(lax.rem(seg + i, 8), chain, blk), device_id_type=MESH)
    for i in range(8):
        pl.semaphore_signal(barrier, inc=1, device_id=peer(seg, lax.rem(chain + i, 8), 1 - blk), device_id_type=MESH)

    load_c = pltpu.make_async_copy(coup_ref.at[:, lb], cbuf, local_sem.at[0])
    load_c.start()
    load_v = pltpu.make_async_copy(vw_ref, vw, local_sem.at[1])
    load_g = pltpu.make_async_copy(gw_ref, gw, local_sem.at[2])
    load_v.start()
    load_g.start()

    for r in range(2):
        row = jnp.broadcast_to(steps_ref[r : r + 1, :], (16, 16))
        col = jnp.sum(jnp.where(iota((16, 16), 0) == iota((16, 16), 1), row, 0.0), axis=1, keepdims=True)
        pack[r, :, :] = jnp.zeros((16, L), F32)
        pack[r, :, 0:16] = inc_ref[r]
        pack[r, :, 16:17] = col
    gbuf[pl.ds(blk, 1)] = gain_ref[...][None]

    pl.semaphore_wait(barrier, 22)

    def inc_copy(i):
        k = lax.rem(chain + i, 8)
        return pltpu.make_async_remote_copy(
            src_ref=pack.at[k // 4], dst_ref=incbuf.at[chain], send_sem=inc_ss.at[i], recv_sem=inc_rs.at[8 - i],
            device_id=peer(seg, k, blk), device_id_type=MESH)

    def gain_copy():
        return pltpu.make_async_remote_copy(
            src_ref=gbuf.at[blk], dst_ref=gbuf.at[blk], send_sem=gain_ss, recv_sem=gain_rs,
            device_id=(tm, 1 - blk), device_id_type=MESH)

    for i in range(1, 8):
        inc_copy(i).start()
    gain_copy().start()
    incbuf[pl.ds(chain, 1)] = pack[pl.ds(rec, 1)]

    decay_row = decay_ref[pl.ds(lb, 1), :]
    dc[0:L, :] = -to_column(decay_row)
    dc[L:ROWS, :] = jnp.zeros((ROWS - L, L), F32)
    load_c.wait()
    for q in range(9):
        if q == 8:
            w = iw_ref[:, pl.ds(pl.multiple_of(lb * L, L), L)]
            wide = jnp.broadcast_to(w[:, None, :], (16, 8, L))
            first = jnp.where(iota((16, 8, L), 1) == 0, wide, 0.0).reshape(L, L)
            second = jnp.zeros((L, L), F32)
            for n, t in enumerate((first, second)):
                hi, lo = split2(t)
                cth[q, 0:L, n * L : (n + 1) * L] = hi
                cth[q, L : 2 * L, n * L : (n + 1) * L] = hi
                ctl[q, :, n * L : (n + 1) * L] = lo

    def transpose_pair(cp, _):
        a = cbuf[2 * cp].T.reshape(16, 8, L)
        b = cbuf[2 * cp + 1].T.reshape(16, 8, L)
        both = jnp.concatenate([a, b], axis=1)
        hi, lo = split2(both)
        base = pl.multiple_of(cp * 16, 16)
        for jb in range(16):
            q, n = jb // 2, jb % 2
            cth[q, pl.ds(base, 16), n * L : (n + 1) * L] = hi[jb]
            cth[q, pl.ds(base + L, 16), n * L : (n + 1) * L] = hi[jb]
            ctl[q, pl.ds(base, 16), n * L : (n + 1) * L] = lo[jb]
        return 0

    lax.fori_loop(0, 8, transpose_pair, 0)

    for i in range(1, 8):
        inc_copy(i).wait_recv()

    incp = incbuf[...].reshape(L, L)
    spread = (iota((L, L), 0) == iota((L, L), 1) // 8).astype(BF16)
    keep = (iota((8, L), 0) == lax.rem(iota((8, L), 1), 8))[None]
    for n, piece in enumerate(split2(incp)):
        wide = mm(piece, spread)
        x = jnp.where(keep, jnp.broadcast_to(wide[:, None, :], (L, 8, L)), 0.0)
        xbuf[:, n * L : (n + 1) * L] = x.reshape(8 * L, L).astype(BF16)

    stepbc = jnp.broadcast_to(incp[:, 16:17], (L, L))
    t_row, t_col = iota((L, L), 0), iota((L, L), 1)
    same = (t_row // 8) == (t_col // 8)
    sig[...] = exact_mask_sum((same & (t_col < t_row)).astype(BF16), stepbc)
    arow[...] = jnp.exp(-stepbc * decay_row)
    prow[...] = jnp.exp(-exact_mask_sum((same & (t_col <= t_row)).astype(BF16), stepbc) * decay_row)
    n_row, n_col = iota((NODES, L), 0), iota((NODES, L), 1)
    low, size = n_row * 8, 8 + 0 * n_row
    for first, width in ((16, 16), (24, 32), (28, 64), (30, 128)):
        low = jnp.where(n_row >= first, (n_row - first) * width, low)
        size = jnp.where(n_row >= first, width, size)
    low = jnp.where(n_row >= 32, 0, low)
    size = jnp.where(n_row >= 32, (n_row - 32) * 8, size)
    sums = exact_mask_sum(((n_col >= low) & (n_col < low + size)).astype(BF16), stepbc)
    ns[...] = sums
    na[...] = jnp.exp(-sums * decay_row)

    def build(q, _):
        rows = 512
        for m in range(8 * L // rows):
            x = xbuf[m * rows : (m + 1) * rows, :]
            e = mm(x, cth[q]) + mm(x[:, :L], ctl[q])
            nt = rows // 8
            t0 = m * nt
            s = sig[t0 : t0 + nt, :][:, None, :]
            base = pl.multiple_of(q * 16, 16)
            pieces = []
            for n in range(2):
                en = e[:, n * L : (n + 1) * L].reshape(nt, 8, L)
                d = dc[pl.ds(base + 8 * n, 8), :][None]
                dbuf[t0 : t0 + nt, pl.ds(base + 8 * n, 8), :] = en * jnp.exp(d * s)
                pieces.append(en)
            eb[t0 : t0 + nt, pl.ds(base, 16), :] = jnp.concatenate(pieces, axis=1).astype(BF16)
        return 0

    lax.fori_loop(0, 9, build, 0)

    def advance(l, _):
        def run(gq, _):
            for gi in range(4):
                t = (gq * 4 + gi) * 8 + l
                d = dbuf[t - 1]
                dbuf[t] = dbuf[t] + d * arow[pl.ds(t, 1), :] + mm(d.astype(BF16), eb[t, 0:L, :])
            return 0

        return lax.fori_loop(0, 4, run, 0)

    lax.fori_loop(1, 8, advance, 0)

    def compose(d1, n1, d2, n2):
        scale = jnp.exp(dc[...] * ns[n1 : n1 + 1, :])
        return scale * d2 + d1 * na[n2 : n2 + 1, :] + mm(d1.astype(BF16), d2[0:L].astype(BF16))

    first_of = (0, 16, 24, 28, 30)

    def node(level, i):
        return dbuf[8 * i + 7] if level == 0 else tree[first_of[level] - 16 + i]

    for level in range(1, 5):
        for i in range(16 >> level):
            tree[first_of[level] - 16 + i] = compose(
                node(level - 1, 2 * i), first_of[level - 1] + 2 * i,
                node(level - 1, 2 * i + 1), first_of[level - 1] + 2 * i + 1)

    whole = tree[14]
    init = h0_ref[:, pl.ds(pl.multiple_of(lb * L, L), L)]
    init = jnp.where(rec == 0, init[0:1], init[1:2])

    def apply_map(h, d_bf, a, v):
        hi, mid, lo = split3(h)
        rid = iota((16, L), 0)
        x = jnp.where(rid == 0, hi.astype(F32), jnp.where(rid == 1, mid.astype(F32), jnp.where(rid == 2, lo.astype(F32), 0.0)))
        return h * a + v + jnp.sum(mm(x.astype(BF16), d_bf), axis=0, keepdims=True)

    top = whole[0:L]
    a_all, v_all = na[30:31, :], whole[L : L + 1]
    msg[0:L, :] = top.astype(BF16)
    after = init * a_all + v_all + jnp.sum(to_column(init) * top, axis=0, keepdims=True)
    v_all = jnp.where(seg == 0, after, v_all)
    rid = iota((16, L), 0)
    tail = jnp.zeros((16, L), F32)
    for n, piece in enumerate(split3(a_all) + split3(v_all)):
        tail = jnp.where(rid == n, jnp.broadcast_to(piece.astype(F32), (16, L)), tail)
    msg[L:ROWS, :] = tail.astype(BF16)

    def map_copy(dst):
        return pltpu.make_async_remote_copy(
            src_ref=msg, dst_ref=maps.at[seg], send_sem=map_ss.at[dst], recv_sem=map_rs.at[seg],
            device_id=peer(dst, chain, blk), device_id_type=MESH)

    def map_arrival(src):
        return pltpu.make_async_remote_copy(
            src_ref=msg, dst_ref=maps.at[src], send_sem=map_ss.at[src], recv_sem=map_rs.at[src],
            device_id=peer(src, chain, blk), device_id_type=MESH)

    def send_map(dst, _):
        map_copy(dst).start()
        return 0

    lax.fori_loop(seg + 1, 8, send_map, 0)

    pref[1] = node(0, 0)
    pref[2] = node(1, 0)
    pref[4] = node(2, 0)
    pref[8] = node(3, 0)
    for dst, a, level, i in (
        (12, 8, 2, 2), (6, 4, 1, 2), (10, 8, 1, 4), (14, 12, 1, 6), (3, 2, 0, 2), (5, 4, 0, 4), (7, 6, 0, 6),
        (9, 8, 0, 8), (11, 10, 0, 10), (13, 12, 0, 12), (15, 14, 0, 14)):
        pref[dst] = compose(pref[a], 32 + a, node(level, i), first_of[level] + i)

    def arrive(src, h):
        map_arrival(src).wait_recv()
        tail = maps[src, L:ROWS, :].astype(F32)
        a = tail[0:1] + tail[1:2] + tail[2:3]
        v = tail[3:4] + tail[4:5] + tail[5:6]
        return jnp.where(src == 0, v, apply_map(h, maps[src, 0:L, :], a, v))

    entry = lax.fori_loop(0, seg, arrive, init)

    ones = (iota((16, L), 0) == 0).astype(F32)
    entry_col = jnp.concatenate([to_column(entry), ones], axis=0)

    def from_start(h, col, d, a):
        return h * a + jnp.sum(col * d, axis=0, keepdims=True)

    for g in range(16):
        hg = entry if g == 0 else from_start(entry, entry_col, pref[g], na[32 + g : 33 + g, :])
        col = jnp.concatenate([to_column(hg), ones], axis=0)
        for l in range(8):
            t = 8 * g + l
            stout[t // 16, t % 16 : t % 16 + 1, :] = from_start(hg, col, dbuf[t], prow[t : t + 1, :])

    def st_copy(i):
        k = lax.rem(chain + i, 8)
        core = blk if i < 8 else 1 - blk
        return pltpu.make_async_remote_copy(
            src_ref=stout.at[k], dst_ref=stbuf.at[blk, chain], send_sem=st_ss.at[i],
            recv_sem=st_rs.at[(8 - i if i < 8 else 8 + (16 - i) % 8)],
            device_id=peer(seg, k, core), device_id_type=MESH)

    def st_arrival(i):
        k = lax.rem(chain + i, 8)
        core = blk if i < 8 else 1 - blk
        return pltpu.make_async_remote_copy(
            src_ref=stout.at[k], dst_ref=stbuf.at[core, k], send_sem=st_ss.at[i], recv_sem=st_rs.at[i],
            device_id=peer(seg, k, core), device_id_type=MESH)

    for i in range(1, 16):
        st_copy(i).start()
    stbuf[pl.ds(blk, 1), pl.ds(chain, 1)] = stout[pl.ds(chain, 1)][None]
    load_v.wait()
    load_g.wait()
    gain_copy().wait_recv()
    for i in range(1, 16):
        st_arrival(i).wait_recv()

    squares = jnp.zeros((32, 1), F32)
    scaled = []
    for core in range(2):
        for b in range(4):
            part = jnp.concatenate([stbuf[core, b], stbuf[core, 4 + b]], axis=0)
            squares = squares + jnp.sum(part * part, axis=1, keepdims=True)
            scaled.append((part * gbuf[core, b : b + 1, :]).astype(BF16))
    scaled = jnp.concatenate(scaled, axis=1)
    inverse = lax.rsqrt(squares / UNITS + 1e-06)
    value = mm(scaled, vw[...]) * inverse
    gate = mm(scaled, gw[...]) * inverse
    out = (value * jax.nn.sigmoid(gate)).astype(BF16)
    read_ref[...] = out.reshape(2, 16, 512)
    own = stbuf[pl.ds(blk, 1)][0]
    for r in range(2):
        for b in range(4):
            states_ref[r, :, b * L : (b + 1) * L] = own[4 * r + b]

    for i in range(1, 8):
        inc_copy(i).wait_send()
    gain_copy().wait_send()

    def sent_map(dst, _):
        map_copy(dst).wait_send()
        return 0

    lax.fori_loop(seg + 1, 8, sent_map, 0)
    for i in range(1, 16):
        st_copy(i).wait_send()


def body(initial_state, decay_rate, step_sizes, increments, coupling, input_weight, gain, value_weight, gate_weight):
    vmem, anyspace = pl.BlockSpec(memory_space=pltpu.VMEM), pl.BlockSpec(memory_space=pl.ANY)
    dma = pltpu.SemaphoreType.DMA
    return pl.pallas_call(
        kernel,
        out_shape=(jax.ShapeDtypeStruct((2, 16, 512), F32), jax.ShapeDtypeStruct((2, 16, 512), BF16)),
        in_specs=[vmem, vmem, vmem, vmem, anyspace, vmem, vmem, anyspace, anyspace],
        out_specs=(vmem, vmem),
        scratch_shapes=[
            pltpu.VMEM((2, 16, L), F32),
            pltpu.VMEM((8, 16, L), F32),
            pltpu.VMEM((16, L, L), F32),
            pltpu.VMEM((1024, 512), BF16),
            pltpu.VMEM((1024, 512), BF16),
            pltpu.VMEM((2, 4, L), F32),
            pltpu.VMEM((9, 2 * L, 2 * L), BF16),
            pltpu.VMEM((9, L, 2 * L), BF16),
            pltpu.VMEM((8 * L, 2 * L), BF16),
            pltpu.VMEM((ROWS, L), F32),
            pltpu.VMEM((L, L), F32),
            pltpu.VMEM((L, L), F32),
            pltpu.VMEM((L, L), F32),
            pltpu.VMEM((NODES, L), F32),
            pltpu.VMEM((NODES, L), F32),
            pltpu.VMEM((L, ROWS, L), F32),
            pltpu.VMEM((L, ROWS, L), BF16),
            pltpu.VMEM((15, ROWS, L), F32),
            pltpu.VMEM((16, ROWS, L), F32),
            pltpu.VMEM((ROWS, L), BF16),
            pltpu.VMEM((8, ROWS, L), BF16),
            pltpu.VMEM((8, 16, L), F32),
            pltpu.VMEM((2, 8, 16, L), F32),
            dma((3,)), dma((8,)), dma((8,)), dma, dma, dma((8,)), dma((8,)), dma((16,)), dma((16,)),
        ],
        compiler_params=pltpu.CompilerParams(
            collective_id=0, has_side_effects=True, vmem_limit_bytes=48 * 1024 * 1024),
        cost_estimate=pl.CostEstimate(flops=10**9, bytes_accessed=4 * 10**6, transcendentals=0),
    )(initial_state, decay_rate.reshape(4, L), step_sizes, increments, coupling, input_weight, gain.reshape(4, L),
      value_weight, gate_weight)


def solution(mesh):
    placed = (
        P(None, "blk"), P("blk"), P(None, "tm"), P(None, "tm", None), P(None, "blk", None, None),
        P(None, "blk"), P("blk"), P(None, "blk"), P(None, "blk"),
    )
    return jax.shard_map(
        body, mesh=mesh, in_specs=placed, out_specs=(P(None, "tm", "blk"), P(None, "tm", "blk")), check_vma=False)
```

profile of v0, /device:TPU:7, one launch (start us, length us, event | category | flops | bytes accessed | tf_op | source)
XLA Modules:
  0.0 53.8 jit_solution(17481329903828867808)
XLA Ops:
  0.6 0.0 copy-start
  0.6 1.2 %copy-done = bf16[1024,512]{1,0:T(8,128)(2,1)S(1)} copy-done((bf16[1024,512]{1,0:T(8,128)(2,1)S(1)}, bf16[1024,512]{1,0:T(8,128)(2,1)}, u32[]{:S(2)}) %copy-start) | copy-done | bytes 1048600
  1.9 0.0 copy-start.1
  1.9 1.2 %copy-done.1 = bf16[1024,512]{1,0:T(8,128)(2,1)S(1)} copy-done((bf16[1024,512]{1,0:T(8,128)(2,1)S(1)}, bf16[1024,512]{1,0:T(8,128)(2,1)}, u32[]{:S(2)}) %copy-start.1) | copy-done | bytes 1048600
  3.1 0.0 copy-start.2
  3.1 0.8 %copy-done.2 = f32[16,512]{1,0:T(8,128)S(1)} copy-done((f32[16,512]{1,0:T(8,128)S(1)}, f32[16,512]{1,0:T(8,128)}, u32[]{:S(2)}) %copy-start.2) | copy-done | bytes 32792
  3.8 0.0 copy-start.3
  3.8 0.7 %copy-done.3 = f32[2,16,16]{2,1,0:T(8,128)S(1)} copy-done((f32[2,16,16]{2,1,0:T(8,128)S(1)}, f32[2,16,16]{2,1,0:T(8,128)}, u32[]{:S(2)}) %copy-start.3) | copy-done | bytes 2072
  4.6 0.0 copy-start.4
  4.6 0.7 %copy-done.4 = f32[2,512]{1,0:T(2,128)S(1)} copy-done((f32[2,512]{1,0:T(2,128)S(1)}, f32[2,512]{1,0:T(2,128)}, u32[]{:S(2)}) %copy-start.4) | copy-done | bytes 4120
  5.2 0.0 copy-start.5
  5.2 0.7 %copy-done.5 = f32[512]{0:T(512)S(1)} copy-done((f32[512]{0:T(512)S(1)}, f32[512]{0:T(512)}, u32[]{:S(2)}) %copy-start.5) | copy-done | bytes 2072
  5.9 0.0 copy-start.6
  5.9 0.7 %copy-done.6 = f32[512]{0:T(512)S(1)} copy-done((f32[512]{0:T(512)S(1)}, f32[512]{0:T(512)}, u32[]{:S(2)}) %copy-start.6) | copy-done | bytes 2072
  6.6 0.0 copy-start.7
  6.6 0.7 %copy-done.7 = f32[2,16]{1,0:T(2,128)S(1)} copy-done((f32[2,16]{1,0:T(2,128)S(1)}, f32[2,16]{1,0:T(2,128)}, u32[]{:S(2)}) %copy-start.7) | copy-done | bytes 152
  7.3 45.2 %shard_map.104 = (f32[2,16,512]{2,1,0:T(8,128)S(1)}, bf16[2,16,512]{2,1,0:T(8,128)(2,1)S(1)}) custom-call(f32[2,512]{1,0:T(2,128)S(1)} %copy-done.4, f32[4,128]{1,0:T(4,128)S(1)} %bitcast.2, f32[2,16]{1,0:T(2,128)S(1)} %copy-done.7, f32[2,16,16]{2,1,0:T(8,128)S(1)} %copy-done.3, f32[16,4,128,128]{3,2,1,0:T(8,128)} %coup_ref.1, f32[16,512]{1,0:T(8,128)S(1)} %copy-done.2, ...), custom_call_target="tpu_custom_call" | custom-call | flops 1000000000 | bytes 4000000 | tf_op jit(solution)/shard_map/pallas_call | solution.py:338
  52.5 0.6 %copy.13 = f32[2,16,512]{2,1,0:T(8,128)} copy(f32[2,16,512]{2,1,0:T(8,128)S(1)} %get-tuple-element.4) | data formatting | bytes 131072
  53.2 0.6 %copy.14 = bf16[2,16,512]{2,1,0:T(8,128)(2,1)} copy(bf16[2,16,512]{2,1,0:T(8,128)(2,1)S(1)} %get-tuple-element.5) | data formatting | bytes 65536
Async XLA Ops:
  0.6 1.2 %copy-start = (bf16[1024,512]{1,0:T(8,128)(2,1)S(1)}, bf16[1024,512]{1,0:T(8,128)(2,1)}, u32[]{:S(2)}) copy-start(bf16[1024,512]{1,0:T(8,128)(2,1)} %vw_ref.1) | copy-start | bytes 3145732
  1.9 1.2 %copy-start.1 = (bf16[1024,512]{1,0:T(8,128)(2,1)S(1)}, bf16[1024,512]{1,0:T(8,128)(2,1)}, u32[]{:S(2)}) copy-start(bf16[1024,512]{1,0:T(8,128)(2,1)} %gw_ref.1) | copy-start | bytes 3145732
  3.1 0.8 %copy-start.2 = (f32[16,512]{1,0:T(8,128)S(1)}, f32[16,512]{1,0:T(8,128)}, u32[]{:S(2)}) copy-start(f32[16,512]{1,0:T(8,128)} %iw_ref.1) | copy-start | bytes 98308
  3.8 0.7 %copy-start.3 = (f32[2,16,16]{2,1,0:T(8,128)S(1)}, f32[2,16,16]{2,1,0:T(8,128)}, u32[]{:S(2)}) copy-start(f32[2,16,16]{2,1,0:T(8,128)} %inc_ref.1) | copy-start | bytes 6148
  4.6 0.7 %copy-start.4 = (f32[2,512]{1,0:T(2,128)S(1)}, f32[2,512]{1,0:T(2,128)}, u32[]{:S(2)}) copy-start(f32[2,512]{1,0:T(2,128)} %h0_ref.1) | copy-start | bytes 12292
  5.2 0.7 %copy-start.5 = (f32[512]{0:T(512)S(1)}, f32[512]{0:T(512)}, u32[]{:S(2)}) copy-start(f32[512]{0:T(512)} %param.10) | copy-start | bytes 6148
  5.9 0.7 %copy-start.6 = (f32[512]{0:T(512)S(1)}, f32[512]{0:T(512)}, u32[]{:S(2)}) copy-start(f32[512]{0:T(512)} %param.15) | copy-start | bytes 6148
  6.6 0.7 %copy-start.7 = (f32[2,16]{1,0:T(2,128)S(1)}, f32[2,16]{1,0:T(2,128)}, u32[]{:S(2)}) copy-start(f32[2,16]{1,0:T(2,128)} %steps_ref.1) | copy-start | bytes 388
where the time goes:
time: 54.6 us; the launch traced here: 53.8 us
  Pallas kernels  45.2 us (83%)
  local copies, waits for them, and re-layouts  7.89 us (14%)
  between operations  0.66 us (1%)
    pallas_call x1, Pallas kernels, body(): pl.pallas_call(kernel, out_shape=(jax.ShapeDtypeStruct((2, 16, 512), F32)...  45.2 us
    unnamed x18, local copies, waits for them, and re-layouts  7.89 us

commit v1 on v0

--- a/solution.py
+++ b/solution.py
@@ -50,9 +50,9 @@
 
 
 def kernel(
-    h0_ref, decay_ref, steps_ref, inc_ref, coup_ref, iw_ref, gain_ref, vw_ref, gw_ref,
+    h0_hbm, decay_hbm, steps_hbm, inc_hbm, coup_hbm, iw_hbm, gain_hbm, vw_hbm, gw_hbm,
     states_ref, read_ref,
-    pack, incbuf, cbuf, vw, gw, gbuf, cth, ctl, xbuf, dc, sig, arow, prow, ns, na,
+    h0_ref, decay_ref, steps_ref, inc_ref, iw_ref, pack, incbuf, cbuf, vw, gw, gbuf, cth, ctl, xbuf, dc, sig, arow, prow, ns, na,
     dbuf, eb, tree, pref, msg, maps, stout, stbuf,
     local_sem, inc_ss, inc_rs, gain_ss, gain_rs, map_ss, map_rs, st_ss, st_rs,
 ):
@@ -70,12 +70,17 @@
     for i in range(8):
         pl.semaphore_signal(barrier, inc=1, device_id=peer(seg, lax.rem(chain + i, 8), 1 - blk), device_id_type=MESH)
 
-    load_c = pltpu.make_async_copy(coup_ref.at[:, lb], cbuf, local_sem.at[0])
-    load_c.start()
-    load_v = pltpu.make_async_copy(vw_ref, vw, local_sem.at[1])
-    load_g = pltpu.make_async_copy(gw_ref, gw, local_sem.at[2])
-    load_v.start()
-    load_g.start()
+    loads = [
+        pltpu.make_async_copy(src, dst, local_sem.at[n])
+        for n, (src, dst) in enumerate((
+            (inc_hbm, inc_ref), (steps_hbm, steps_ref), (gain_hbm, gbuf.at[blk]), (decay_hbm, decay_ref),
+            (iw_hbm, iw_ref), (h0_hbm, h0_ref), (coup_hbm.at[:, lb], cbuf), (vw_hbm, vw), (gw_hbm, gw)))
+    ]
+    load_inc, load_steps, load_gain, load_decay, load_iw, load_h0, load_c, load_v, load_g = loads
+    for load in loads:
+        load.start()
+    load_inc.wait()
+    load_steps.wait()
 
     for r in range(2):
         row = jnp.broadcast_to(steps_ref[r : r + 1, :], (16, 16))
@@ -83,7 +88,7 @@
         pack[r, :, :] = jnp.zeros((16, L), F32)
         pack[r, :, 0:16] = inc_ref[r]
         pack[r, :, 16:17] = col
-    gbuf[pl.ds(blk, 1)] = gain_ref[...][None]
+    load_gain.wait()
 
     pl.semaphore_wait(barrier, 22)
 
@@ -103,6 +108,9 @@
     gain_copy().start()
     incbuf[pl.ds(chain, 1)] = pack[pl.ds(rec, 1)]
 
+    load_decay.wait()
+    load_iw.wait()
+    load_h0.wait()
     decay_row = decay_ref[pl.ds(lb, 1), :]
     dc[0:L, :] = -to_column(decay_row)
     dc[L:ROWS, :] = jnp.zeros((ROWS - L, L), F32)
@@ -182,17 +190,11 @@
 
     lax.fori_loop(0, 9, build, 0)
 
-    def advance(l, _):
-        def run(gq, _):
-            for gi in range(4):
-                t = (gq * 4 + gi) * 8 + l
-                d = dbuf[t - 1]
-                dbuf[t] = dbuf[t] + d * arow[pl.ds(t, 1), :] + mm(d.astype(BF16), eb[t, 0:L, :])
-            return 0
-
-        return lax.fori_loop(0, 4, run, 0)
-
-    lax.fori_loop(1, 8, advance, 0)
+    for l in range(1, 8):
+        for g in range(16):
+            t = 8 * g + l
+            d = dbuf[t - 1]
+            dbuf[t] = dbuf[t] + d * arow[t : t + 1, :] + mm(d.astype(BF16), eb[t, 0:L, :])
 
     def compose(d1, n1, d2, n2):
         scale = jnp.exp(dc[...] * ns[n1 : n1 + 1, :])
@@ -333,14 +335,19 @@
 
 
 def body(initial_state, decay_rate, step_sizes, increments, coupling, input_weight, gain, value_weight, gate_weight):
-    vmem, anyspace = pl.BlockSpec(memory_space=pltpu.VMEM), pl.BlockSpec(memory_space=pl.ANY)
+    vmem, hbm = pl.BlockSpec(memory_space=pltpu.VMEM), pl.BlockSpec(memory_space=pltpu.HBM)
     dma = pltpu.SemaphoreType.DMA
     return pl.pallas_call(
         kernel,
         out_shape=(jax.ShapeDtypeStruct((2, 16, 512), F32), jax.ShapeDtypeStruct((2, 16, 512), BF16)),
-        in_specs=[vmem, vmem, vmem, vmem, anyspace, vmem, vmem, anyspace, anyspace],
+        in_specs=[hbm] * 9,
         out_specs=(vmem, vmem),
         scratch_shapes=[
+            pltpu.VMEM((2, 512), F32),
+            pltpu.VMEM((4, L), F32),
+            pltpu.VMEM((2, 16), F32),
+            pltpu.VMEM((2, 16, 16), F32),
+            pltpu.VMEM((16, 512), F32),
             pltpu.VMEM((2, 16, L), F32),
             pltpu.VMEM((8, 16, L), F32),
             pltpu.VMEM((16, L, L), F32),
@@ -364,10 +371,10 @@
             pltpu.VMEM((8, ROWS, L), BF16),
             pltpu.VMEM((8, 16, L), F32),
             pltpu.VMEM((2, 8, 16, L), F32),
-            dma((3,)), dma((8,)), dma((8,)), dma, dma, dma((8,)), dma((8,)), dma((16,)), dma((16,)),
+            dma((9,)), dma((8,)), dma((8,)), dma, dma, dma((8,)), dma((8,)), dma((16,)), dma((16,)),
         ],
         compiler_params=pltpu.CompilerParams(
-            collective_id=0, has_side_effects=True, vmem_limit_bytes=48 * 1024 * 1024),
+            collective_id=0, has_side_effects=True, vmem_limit_bytes=60 * 1024 * 1024),
         cost_estimate=pl.CostEstimate(flops=10**9, bytes_accessed=4 * 10**6, transcendentals=0),
     )(initial_state, decay_rate.reshape(4, L), step_sizes, increments, coupling, input_weight, gain.reshape(4, L),
       value_weight, gate_weight)

time: 54.6 us -> 34.8 us (0.64)
  Pallas kernels: 45.2 us -> 30.6 us
  local copies, waits for them, and re-layouts: 7.89 us -> 2.85 us
    pallas_call x1, Pallas kernels: 45.2 us -> 30.6 us  [body(): pl.pallas_call(kernel, out_shape=(jax.ShapeDtypeStruct((2, 16, 512), F32)...]
    unnamed x18 -> x2, local copies, waits for them, and re-layouts: 7.89 us -> 2.85 us
where the time goes in v1:
time: 34.8 us; the launch traced here: 34.1 us
  Pallas kernels  30.6 us (88%)
  local copies, waits for them, and re-layouts  2.85 us (8%)
  between operations  0.64 us (2%)
    pallas_call x1, Pallas kernels, body(): pl.pallas_call(kernel, out_shape=(jax.ShapeDtypeStruct((2, 16, 512), F32)...  30.6 us
    unnamed x2, local copies, waits for them, and re-layouts  2.85 us

profile of v1, /device:TPU:7, one launch (start us, length us, event | category | flops | bytes accessed | tf_op | source)
XLA Modules:
  0.0 34.1 jit_solution(16040074920251838128)
XLA Ops:
  0.6 30.6 %shard_map.104 = (f32[2,16,512]{2,1,0:T(8,128)}, bf16[2,16,512]{2,1,0:T(8,128)(2,1)}) custom-call(f32[2,512]{1,0:T(2,128)} %h0_hbm.1, f32[4,128]{1,0:T(4,128)} %bitcast.2, f32[2,16]{1,0:T(2,128)} %steps_hbm.1, f32[2,16,16]{2,1,0:T(8,128)} %inc_hbm.1, f32[16,4,128,128]{3,2,1,0:T(8,128)} %coup_hbm.1, f32[16,512]{1,0:T(8,128)} %iw_hbm.1, f32[4,128]{1,0:T(4,128)} %bitcast.3, ...), custom_call_target="tpu_custom_call" | custom-call | flops 1000000000 | bytes 4000000 | tf_op jit(solution)/shard_map/pallas_call | solution.py:340
  31.3 1.5 %copy.13 = f32[2,16,512]{2,1,0:T(8,128)} copy(f32[2,16,512]{2,1,0:T(8,128)} %get-tuple-element.4) | data formatting | bytes 131072
  32.8 1.4 %copy.14 = bf16[2,16,512]{2,1,0:T(8,128)(2,1)} copy(bf16[2,16,512]{2,1,0:T(8,128)(2,1)} %get-tuple-element.5) | data formatting | bytes 65536

commit v2 on v1

--- a/solution.py
+++ b/solution.py
@@ -63,13 +63,6 @@
     def peer(s, k, c):
         return (s * 8 + k, c)
 
-    barrier = pltpu.get_barrier_semaphore()
-    for i in range(1, 8):
-        pl.semaphore_signal(barrier, inc=1, device_id=peer(seg, lax.rem(chain + i, 8), blk), device_id_type=MESH)
-        pl.semaphore_signal(barrier, inc=1, device_id=peer(lax.rem(seg + i, 8), chain, blk), device_id_type=MESH)
-    for i in range(8):
-        pl.semaphore_signal(barrier, inc=1, device_id=peer(seg, lax.rem(chain + i, 8), 1 - blk), device_id_type=MESH)
-
     loads = [
         pltpu.make_async_copy(src, dst, local_sem.at[n])
         for n, (src, dst) in enumerate((
@@ -79,6 +72,13 @@
     load_inc, load_steps, load_gain, load_decay, load_iw, load_h0, load_c, load_v, load_g = loads
     for load in loads:
         load.start()
+    barrier = pltpu.get_barrier_semaphore()
+    for i in range(1, 8):
+        pl.semaphore_signal(barrier, inc=1, device_id=peer(seg, lax.rem(chain + i, 8), blk), device_id_type=MESH)
+        pl.semaphore_signal(barrier, inc=1, device_id=peer(lax.rem(seg + i, 8), chain, blk), device_id_type=MESH)
+    for i in range(8):
+        pl.semaphore_signal(barrier, inc=1, device_id=peer(seg, lax.rem(chain + i, 8), 1 - blk), device_id_type=MESH)
+
     load_inc.wait()
     load_steps.wait()
 
@@ -95,7 +95,7 @@
     def inc_copy(i):
         k = lax.rem(chain + i, 8)
         return pltpu.make_async_remote_copy(
-            src_ref=pack.at[k // 4], dst_ref=incbuf.at[chain], send_sem=inc_ss.at[i], recv_sem=inc_rs.at[8 - i],
+            src_ref=pack.at[k // 4], dst_ref=incbuf.at[pl.ds(chain * 16, 16)], send_sem=inc_ss.at[i], recv_sem=inc_rs.at[8 - i],
             device_id=peer(seg, k, blk), device_id_type=MESH)
 
     def gain_copy():
@@ -106,7 +106,7 @@
     for i in range(1, 8):
         inc_copy(i).start()
     gain_copy().start()
-    incbuf[pl.ds(chain, 1)] = pack[pl.ds(rec, 1)]
+    incbuf[pl.ds(pl.multiple_of(chain * 16, 16), 16), :] = pack[rec]
 
     load_decay.wait()
     load_iw.wait()
@@ -145,7 +145,7 @@
     for i in range(1, 8):
         inc_copy(i).wait_recv()
 
-    incp = incbuf[...].reshape(L, L)
+    incp = jnp.concatenate([incbuf[pl.ds(l, 16, stride=8), :] for l in range(8)], axis=0)
     spread = (iota((L, L), 0) == iota((L, L), 1) // 8).astype(BF16)
     keep = (iota((8, L), 0) == lax.rem(iota((8, L), 1), 8))[None]
     for n, piece in enumerate(split2(incp)):
@@ -155,11 +155,12 @@
 
     stepbc = jnp.broadcast_to(incp[:, 16:17], (L, L))
     t_row, t_col = iota((L, L), 0), iota((L, L), 1)
-    same = (t_row // 8) == (t_col // 8)
+    same = lax.rem(t_row, 16) == lax.rem(t_col, 16)
     sig[...] = exact_mask_sum((same & (t_col < t_row)).astype(BF16), stepbc)
     arow[...] = jnp.exp(-stepbc * decay_row)
     prow[...] = jnp.exp(-exact_mask_sum((same & (t_col <= t_row)).astype(BF16), stepbc) * decay_row)
     n_row, n_col = iota((NODES, L), 0), iota((NODES, L), 1)
+    n_col = lax.rem(n_col, 16) * 8 + n_col // 16
     low, size = n_row * 8, 8 + 0 * n_row
     for first, width in ((16, 16), (24, 32), (28, 64), (30, 128)):
         low = jnp.where(n_row >= first, (n_row - first) * width, low)
@@ -170,32 +171,6 @@
     ns[...] = sums
     na[...] = jnp.exp(-sums * decay_row)
 
-    def build(q, _):
-        rows = 512
-        for m in range(8 * L // rows):
-            x = xbuf[m * rows : (m + 1) * rows, :]
-            e = mm(x, cth[q]) + mm(x[:, :L], ctl[q])
-            nt = rows // 8
-            t0 = m * nt
-            s = sig[t0 : t0 + nt, :][:, None, :]
-            base = pl.multiple_of(q * 16, 16)
-            pieces = []
-            for n in range(2):
-                en = e[:, n * L : (n + 1) * L].reshape(nt, 8, L)
-                d = dc[pl.ds(base + 8 * n, 8), :][None]
-                dbuf[t0 : t0 + nt, pl.ds(base + 8 * n, 8), :] = en * jnp.exp(d * s)
-                pieces.append(en)
-            eb[t0 : t0 + nt, pl.ds(base, 16), :] = jnp.concatenate(pieces, axis=1).astype(BF16)
-        return 0
-
-    lax.fori_loop(0, 9, build, 0)
-
-    for l in range(1, 8):
-        for g in range(16):
-            t = 8 * g + l
-            d = dbuf[t - 1]
-            dbuf[t] = dbuf[t] + d * arow[t : t + 1, :] + mm(d.astype(BF16), eb[t, 0:L, :])
-
     def compose(d1, n1, d2, n2):
         scale = jnp.exp(dc[...] * ns[n1 : n1 + 1, :])
         return scale * d2 + d1 * na[n2 : n2 + 1, :] + mm(d1.astype(BF16), d2[0:L].astype(BF16))
@@ -203,7 +178,38 @@
     first_of = (0, 16, 24, 28, 30)
 
     def node(level, i):
-        return dbuf[8 * i + 7] if level == 0 else tree[first_of[level] - 16 + i]
+        return dbuf[7 * 16 + i] if level == 0 else tree[first_of[level] - 16 + i]
+
+    def build(q, m):
+        rows = 256
+        x = xbuf[m * rows : (m + 1) * rows, :]
+        e = mm(x, cth[q]) + mm(x[:, :L], ctl[q])
+        nt = rows // 8
+        t0, base = m * nt, q * 16
+        s = sig[t0 : t0 + nt, :][:, None, :]
+        pieces = []
+        for n in range(2):
+            en = e[:, n * L : (n + 1) * L].reshape(nt, 8, L)
+            d = dc[base + 8 * n : base + 8 * n + 8, :][None]
+            dbuf[t0 : t0 + nt, base + 8 * n : base + 8 * n + 8, :] = en * jnp.exp(d * s)
+            pieces.append(en)
+        eb[t0 : t0 + nt, base : base + 16, :] = jnp.concatenate(pieces, axis=1).astype(BF16)
+
+    def advance(t):
+        d = dbuf[t - 16]
+        dbuf[t] = dbuf[t] + d * arow[t : t + 1, :] + mm(d.astype(BF16), eb[t, 0:L, :])
+
+    waiting = []
+    for m in range(4):
+        for q in range(9):
+            build(q, m)
+            now = -(-len(waiting) // (9 - q))
+            for t in waiting[:now]:
+                advance(t)
+            waiting = waiting[now:]
+        waiting = list(range(max(16, 32 * m), 32 * m + 32))
+    for t in waiting:
+        advance(t)
 
     for level in range(1, 5):
         for i in range(16 >> level):
@@ -277,7 +283,7 @@
         col = jnp.concatenate([to_column(hg), ones], axis=0)
         for l in range(8):
             t = 8 * g + l
-            stout[t // 16, t % 16 : t % 16 + 1, :] = from_start(hg, col, dbuf[t], prow[t : t + 1, :])
+            stout[t // 16, t % 16 : t % 16 + 1, :] = from_start(hg, col, dbuf[l * 16 + g], prow[l * 16 + g : l * 16 + g + 1, :])
 
     def st_copy(i):
         k = lax.rem(chain + i, 8)
@@ -335,6 +341,9 @@
 
 
 def body(initial_state, decay_rate, step_sizes, increments, coupling, input_weight, gain, value_weight, gate_weight):
+    args = (initial_state, decay_rate.reshape(4, L), step_sizes, increments, coupling, input_weight, gain.reshape(4, L),
+            value_weight, gate_weight)
+    args = [pltpu.with_memory_space_constraint(a, pltpu.HBM) for a in args]
     vmem, hbm = pl.BlockSpec(memory_space=pltpu.VMEM), pl.BlockSpec(memory_space=pltpu.HBM)
     dma = pltpu.SemaphoreType.DMA
     return pl.pallas_call(
@@ -349,7 +358,7 @@
             pltpu.VMEM((2, 16, 16), F32),
             pltpu.VMEM((16, 512), F32),
             pltpu.VMEM((2, 16, L), F32),
-            pltpu.VMEM((8, 16, L), F32),
+            pltpu.VMEM((L, L), F32),
             pltpu.VMEM((16, L, L), F32),
             pltpu.VMEM((1024, 512), BF16),
             pltpu.VMEM((1024, 512), BF16),
@@ -374,10 +383,9 @@
             dma((9,)), dma((8,)), dma((8,)), dma, dma, dma((8,)), dma((8,)), dma((16,)), dma((16,)),
         ],
         compiler_params=pltpu.CompilerParams(
-            collective_id=0, has_side_effects=True, vmem_limit_bytes=60 * 1024 * 1024),
+            collective_id=0, has_side_effects=True, vmem_limit_bytes=48 * 1024 * 1024),
         cost_estimate=pl.CostEstimate(flops=10**9, bytes_accessed=4 * 10**6, transcendentals=0),
-    )(initial_state, decay_rate.reshape(4, L), step_sizes, increments, coupling, input_weight, gain.reshape(4, L),
-      value_weight, gate_weight)
+    )(*args)
 
 
 def solution(mesh):

time: 34.8 us -> 30.9 us (0.89)
  Pallas kernels: 30.6 us -> 28.4 us
  local copies, waits for them, and re-layouts: 2.85 us -> 1.25 us
    pallas_call x1, Pallas kernels: 30.6 us -> 28.4 us  [body(): pl.pallas_call(kernel, out_shape=(jax.ShapeDtypeStruct((2, 16, 512), F32)...]
    unnamed x2, local copies, waits for them, and re-layouts: 2.85 us -> 1.25 us
where the time goes in v2:
time: 30.9 us; the launch traced here: 30.3 us
  Pallas kernels  28.4 us (92%)
  local copies, waits for them, and re-layouts  1.25 us (4%)
  between operations  0.64 us (2%)
    pallas_call x1, Pallas kernels, body(): pl.pallas_call(kernel, out_shape=(jax.ShapeDtypeStruct((2, 16, 512), F32)...  28.4 us
    unnamed x2, local copies, waits for them, and re-layouts  1.25 us

profile of v2, /device:TPU:7, one launch (start us, length us, event | category | flops | bytes accessed | tf_op | source)
XLA Modules:
  0.0 30.3 jit_solution(11774942739859005926)
XLA Ops:
  0.6 28.4 %shard_map.104 = (f32[2,16,512]{2,1,0:T(8,128)S(1)}, bf16[2,16,512]{2,1,0:T(8,128)(2,1)S(1)}) custom-call(f32[2,512]{1,0:T(2,128)} %h0_hbm.1, f32[4,128]{1,0:T(4,128)} %bitcast.2, f32[2,16]{1,0:T(2,128)} %steps_hbm.1, f32[2,16,16]{2,1,0:T(8,128)} %inc_hbm.1, f32[16,4,128,128]{3,2,1,0:T(8,128)} %coup_hbm.1, f32[16,512]{1,0:T(8,128)} %iw_hbm.1, ...), custom_call_target="tpu_custom_call" | custom-call | flops 1000000000 | bytes 4000000 | tf_op jit(solution)/shard_map/pallas_call | solution.py:349
  29.1 0.6 %copy.13 = f32[2,16,512]{2,1,0:T(8,128)} copy(f32[2,16,512]{2,1,0:T(8,128)S(1)} %get-tuple-element.4) | data formatting | bytes 131072
  29.7 0.6 %copy.14 = bf16[2,16,512]{2,1,0:T(8,128)(2,1)} copy(bf16[2,16,512]{2,1,0:T(8,128)(2,1)S(1)} %get-tuple-element.5) | data formatting | bytes 65536

commit v3 on v2

--- a/solution.py
+++ b/solution.py
@@ -13,6 +13,7 @@
 L = 128
 ROWS = 144
 NODES = 48
+AROUND = ((1, 2), (0, 2), (1, 1), (1, 3), (0, 1), (0, 3), (1, 0), (0, 0))
 
 
 def iota(shape, dim):
@@ -53,15 +54,22 @@
     h0_hbm, decay_hbm, steps_hbm, inc_hbm, coup_hbm, iw_hbm, gain_hbm, vw_hbm, gw_hbm,
     states_ref, read_ref,
     h0_ref, decay_ref, steps_ref, inc_ref, iw_ref, pack, incbuf, cbuf, vw, gw, gbuf, cth, ctl, xbuf, dc, sig, arow, prow, ns, na,
-    dbuf, eb, tree, pref, msg, maps, stout, stbuf,
+    dbuf, eb, tree, pref, msg, maps, starts, cols, stout, scout, stbuf, scbuf,
     local_sem, inc_ss, inc_rs, gain_ss, gain_rs, map_ss, map_rs, st_ss, st_rs,
 ):
     tm, blk = lax.axis_index("tm"), lax.axis_index("blk")
-    seg, chain = tm // 8, lax.rem(tm, 8)
+    seg, pos = tm // 8, lax.rem(tm, 8)
+    flip = 4 * lax.rem(seg, 2)
+    chain = lax.rem(pos + flip, 8)
     rec, lb = chain // 4, lax.rem(chain, 4)
 
-    def peer(s, k, c):
-        return (s * 8 + k, c)
+    def holder(s):
+        return (s * 8 + lax.rem(chain + 4 * lax.rem(s, 2), 8), blk)
+
+    def near(i):
+        dy, dz = AROUND[i]
+        p = lax.rem(pos // 4 + dy, 2) * 4 + lax.rem(lax.rem(pos, 4) + dz, 4)
+        return p, lax.rem(p + flip, 8)
 
     loads = [
         pltpu.make_async_copy(src, dst, local_sem.at[n])
@@ -73,12 +81,16 @@
     for load in loads:
         load.start()
     barrier = pltpu.get_barrier_semaphore()
-    for i in range(1, 8):
-        pl.semaphore_signal(barrier, inc=1, device_id=peer(seg, lax.rem(chain + i, 8), blk), device_id_type=MESH)
-        pl.semaphore_signal(barrier, inc=1, device_id=peer(lax.rem(seg + i, 8), chain, blk), device_id_type=MESH)
+    for i in range(7):
+        pl.semaphore_signal(barrier, inc=1, device_id=(seg * 8 + near(i)[0], blk), device_id_type=MESH)
     for i in range(8):
-        pl.semaphore_signal(barrier, inc=1, device_id=peer(seg, lax.rem(chain + i, 8), 1 - blk), device_id_type=MESH)
-
+        pl.semaphore_signal(barrier, inc=1, device_id=(seg * 8 + near(i)[0], 1 - blk), device_id_type=MESH)
+
+    def greet(s, _):
+        pl.semaphore_signal(barrier, inc=1, device_id=holder(s), device_id_type=MESH)
+        return 0
+
+    lax.fori_loop(0, seg, greet, 0)
     load_inc.wait()
     load_steps.wait()
 
@@ -90,23 +102,29 @@
         pack[r, :, 16:17] = col
     load_gain.wait()
 
-    pl.semaphore_wait(barrier, 22)
+    pl.semaphore_wait(barrier, 15 + 7 - seg)
 
     def inc_copy(i):
-        k = lax.rem(chain + i, 8)
+        p, k = near(i)
         return pltpu.make_async_remote_copy(
-            src_ref=pack.at[k // 4], dst_ref=incbuf.at[pl.ds(chain * 16, 16)], send_sem=inc_ss.at[i], recv_sem=inc_rs.at[8 - i],
-            device_id=peer(seg, k, blk), device_id_type=MESH)
+            src_ref=pack.at[k // 4], dst_ref=incbuf.at[pl.ds(pos * 16, 16)], send_sem=inc_ss.at[p], recv_sem=inc_rs.at[pos],
+            device_id=(seg * 8 + p, blk), device_id_type=MESH)
+
+    def inc_arrival(i):
+        p, k = near(i)
+        return pltpu.make_async_remote_copy(
+            src_ref=pack.at[k // 4], dst_ref=incbuf.at[pl.ds(p * 16, 16)], send_sem=inc_ss.at[p], recv_sem=inc_rs.at[p],
+            device_id=(seg * 8 + p, blk), device_id_type=MESH)
 
     def gain_copy():
         return pltpu.make_async_remote_copy(
             src_ref=gbuf.at[blk], dst_ref=gbuf.at[blk], send_sem=gain_ss, recv_sem=gain_rs,
             device_id=(tm, 1 - blk), device_id_type=MESH)
 
-    for i in range(1, 8):
+    for i in range(7):
         inc_copy(i).start()
     gain_copy().start()
-    incbuf[pl.ds(pl.multiple_of(chain * 16, 16), 16), :] = pack[rec]
+    incbuf[pl.ds(pl.multiple_of(pos * 16, 16), 16), :] = pack[rec]
 
     load_decay.wait()
     load_iw.wait()
@@ -142,8 +160,8 @@
 
     lax.fori_loop(0, 8, transpose_pair, 0)
 
-    for i in range(1, 8):
-        inc_copy(i).wait_recv()
+    for i in range(7):
+        inc_arrival(i).wait_recv()
 
     incp = jnp.concatenate([incbuf[pl.ds(l, 16, stride=8), :] for l in range(8)], axis=0)
     spread = (iota((L, L), 0) == iota((L, L), 1) // 8).astype(BF16)
@@ -238,22 +256,30 @@
         tail = jnp.where(rid == n, jnp.broadcast_to(piece.astype(F32), (16, L)), tail)
     msg[L:ROWS, :] = tail.astype(BF16)
 
-    def map_copy(dst):
+    def map_copy(src, dst, rows):
         return pltpu.make_async_remote_copy(
-            src_ref=msg, dst_ref=maps.at[seg], send_sem=map_ss.at[dst], recv_sem=map_rs.at[seg],
-            device_id=peer(dst, chain, blk), device_id_type=MESH)
-
-    def map_arrival(src):
-        return pltpu.make_async_remote_copy(
-            src_ref=msg, dst_ref=maps.at[src], send_sem=map_ss.at[src], recv_sem=map_rs.at[src],
-            device_id=peer(src, chain, blk), device_id_type=MESH)
-
-    def send_map(dst, _):
-        map_copy(dst).start()
-        return 0
-
-    lax.fori_loop(seg + 1, 8, send_map, 0)
-
+            src_ref=msg.at[rows], dst_ref=maps.at[src, rows], send_sem=map_ss.at[dst], recv_sem=map_rs.at[src],
+            device_id=holder(dst), device_id_type=MESH)
+
+    full, last = pl.ds(0, ROWS), pl.ds(L, ROWS - L)
+
+    def to_later(act):
+        def one(n, _):
+            @pl.when(seg == 0)
+            def _():
+                act(map_copy(seg, 7 - n, last))
+
+            @pl.when(seg > 0)
+            def _():
+                act(map_copy(seg, 7 - n, full))
+
+            return 0
+
+        lax.fori_loop(0, 7 - seg, one, 0)
+
+    to_later(lambda copy: copy.start())
+
+    pref[0] = jnp.zeros((ROWS, L), F32)
     pref[1] = node(0, 0)
     pref[2] = node(1, 0)
     pref[4] = node(2, 0)
@@ -263,14 +289,20 @@
         (9, 8, 0, 8), (11, 10, 0, 10), (13, 12, 0, 12), (15, 14, 0, 14)):
         pref[dst] = compose(pref[a], 32 + a, node(level, i), first_of[level] + i)
 
+    def tail_of(src):
+        tail = maps[src, L:ROWS, :].astype(F32)
+        return tail[0:1] + tail[1:2] + tail[2:3], tail[3:4] + tail[4:5] + tail[5:6]
+
+    def begin():
+        map_copy(0, 0, last).wait_recv()
+        return tail_of(0)[1]
+
     def arrive(src, h):
-        map_arrival(src).wait_recv()
-        tail = maps[src, L:ROWS, :].astype(F32)
-        a = tail[0:1] + tail[1:2] + tail[2:3]
-        v = tail[3:4] + tail[4:5] + tail[5:6]
-        return jnp.where(src == 0, v, apply_map(h, maps[src, 0:L, :], a, v))
-
-    entry = lax.fori_loop(0, seg, arrive, init)
+        map_copy(src, src, full).wait_recv()
+        a, v = tail_of(src)
+        return apply_map(h, maps[src, 0:L, :], a, v)
+
+    entry = lax.fori_loop(1, seg, arrive, lax.cond(seg > 0, begin, lambda: init))
 
     ones = (iota((16, L), 0) == 0).astype(F32)
     entry_col = jnp.concatenate([to_column(entry), ones], axis=0)
@@ -280,64 +312,74 @@
 
     for g in range(16):
         hg = entry if g == 0 else from_start(entry, entry_col, pref[g], na[32 + g : 33 + g, :])
-        col = jnp.concatenate([to_column(hg), ones], axis=0)
-        for l in range(8):
-            t = 8 * g + l
-            stout[t // 16, t % 16 : t % 16 + 1, :] = from_start(hg, col, dbuf[l * 16 + g], prow[l * 16 + g : l * 16 + g + 1, :])
-
-    def st_copy(i):
-        k = lax.rem(chain + i, 8)
-        core = blk if i < 8 else 1 - blk
-        return pltpu.make_async_remote_copy(
-            src_ref=stout.at[k], dst_ref=stbuf.at[blk, chain], send_sem=st_ss.at[i],
-            recv_sem=st_rs.at[(8 - i if i < 8 else 8 + (16 - i) % 8)],
-            device_id=peer(seg, k, core), device_id_type=MESH)
-
-    def st_arrival(i):
-        k = lax.rem(chain + i, 8)
-        core = blk if i < 8 else 1 - blk
-        return pltpu.make_async_remote_copy(
-            src_ref=stout.at[k], dst_ref=stbuf.at[core, k], send_sem=st_ss.at[i], recv_sem=st_rs.at[i],
-            device_id=peer(seg, k, core), device_id_type=MESH)
-
-    for i in range(1, 16):
-        st_copy(i).start()
-    stbuf[pl.ds(blk, 1), pl.ds(chain, 1)] = stout[pl.ds(chain, 1)][None]
+        starts[g, 0:1, :] = hg
+        cols[g, 0:L, :] = to_column(hg)
+        cols[g, L:ROWS, :] = ones
+
+    def home(i, p, k):
+        own = pltpu.make_async_remote_copy(
+            src_ref=stout.at[p], dst_ref=stbuf.at[k], send_sem=st_ss.at[p], recv_sem=st_rs.at[k],
+            device_id=(seg * 8 + p, blk), device_id_type=MESH)
+        other = pltpu.make_async_remote_copy(
+            src_ref=scout.at[p], dst_ref=scbuf.at[k], send_sem=st_ss.at[8 + p], recv_sem=st_rs.at[8 + k],
+            device_id=(seg * 8 + p, 1 - blk), device_id_type=MESH)
+        return (own, other) if i < 7 else (other,)
+
+    gain_row = gbuf[blk, pl.ds(lb, 1), :]
+    for i in range(8):
+        p, _ = near(i)
+        for half in range(2):
+            g = 2 * p + half
+            hg, col = starts[g, 0:1, :], cols[g]
+            rows = []
+            for l in range(8):
+                t = l * 16 + g
+                rows.append(from_start(hg, col, dbuf[t], prow[pl.ds(t, 1), :]))
+            stout[p, half * 8 : half * 8 + 8, :] = jnp.concatenate(rows, axis=0)
+        scout[p] = (stout[p] * gain_row).astype(BF16)
+        for copy in home(i, p, chain):
+            copy.start()
+    stbuf[pl.ds(chain, 1)] = stout[pl.ds(pos, 1)]
     load_v.wait()
     load_g.wait()
     gain_copy().wait_recv()
-    for i in range(1, 16):
-        st_arrival(i).wait_recv()
+    for i in range(8):
+        p, k = near(i)
+        for copy in home(i, p, k):
+            copy.wait_recv()
 
     squares = jnp.zeros((32, 1), F32)
-    scaled = []
-    for core in range(2):
-        for b in range(4):
-            part = jnp.concatenate([stbuf[core, b], stbuf[core, 4 + b]], axis=0)
-            squares = squares + jnp.sum(part * part, axis=1, keepdims=True)
-            scaled.append((part * gbuf[core, b : b + 1, :]).astype(BF16))
-    scaled = jnp.concatenate(scaled, axis=1)
+    mine, theirs = [], []
+    other_gain = gbuf[1 - blk]
+    for b in range(4):
+        part = jnp.concatenate([stbuf[b], stbuf[4 + b]], axis=0)
+        squares = squares + jnp.sum(part * part, axis=1, keepdims=True)
+        mine.append((part * gbuf[blk, b : b + 1, :]).astype(BF16))
+        part = jnp.concatenate([scbuf[b], scbuf[4 + b]], axis=0)
+        theirs.append(part)
+        part = part.astype(F32) / other_gain[b : b + 1]
+        squares = squares + jnp.sum(part * part, axis=1, keepdims=True)
+    mine, theirs = jnp.concatenate(mine, axis=1), jnp.concatenate(theirs, axis=1)
+    first = blk == 0
+    scaled = jnp.concatenate([jnp.where(first, mine, theirs), jnp.where(first, theirs, mine)], axis=1)
     inverse = lax.rsqrt(squares / UNITS + 1e-06)
     value = mm(scaled, vw[...]) * inverse
     gate = mm(scaled, gw[...]) * inverse
     out = (value * jax.nn.sigmoid(gate)).astype(BF16)
     read_ref[...] = out.reshape(2, 16, 512)
-    own = stbuf[pl.ds(blk, 1)][0]
     for r in range(2):
         for b in range(4):
-            states_ref[r, :, b * L : (b + 1) * L] = own[4 * r + b]
-
-    for i in range(1, 8):
+            states_ref[r, :, b * L : (b + 1) * L] = stbuf[4 * r + b]
+
+    for i in range(7):
         inc_copy(i).wait_send()
     gain_copy().wait_send()
 
-    def sent_map(dst, _):
-        map_copy(dst).wait_send()
-        return 0
-
-    lax.fori_loop(seg + 1, 8, sent_map, 0)
-    for i in range(1, 16):
-        st_copy(i).wait_send()
+    to_later(lambda copy: copy.wait_send())
+    for i in range(8):
+        p, k = near(i)
+        for copy in home(i, p, k):
+            copy.wait_send()
 
 
 def body(initial_state, decay_rate, step_sizes, increments, coupling, input_weight, gain, value_weight, gate_weight):
@@ -378,8 +420,12 @@
             pltpu.VMEM((16, ROWS, L), F32),
             pltpu.VMEM((ROWS, L), BF16),
             pltpu.VMEM((8, ROWS, L), BF16),
+            pltpu.VMEM((16, 8, L), F32),
+            pltpu.VMEM((16, ROWS, L), F32),
             pltpu.VMEM((8, 16, L), F32),
-            pltpu.VMEM((2, 8, 16, L), F32),
+            pltpu.VMEM((8, 16, L), BF16),
+            pltpu.VMEM((8, 16, L), F32),
+            pltpu.VMEM((8, 16, L), BF16),
             dma((9,)), dma((8,)), dma((8,)), dma, dma, dma((8,)), dma((8,)), dma((16,)), dma((16,)),
         ],
         compiler_params=pltpu.CompilerParams(

time: 30.9 us -> 29.3 us (0.948); the launches traced: 30.3 us -> 29.1 us
  Pallas kernels: 28.4 us -> 27.2 us
    pallas_call x1, Pallas kernels: 28.4 us -> 27.2 us  [body(): pl.pallas_call(kernel, out_shape=(jax.ShapeDtypeStruct((2, 16, 512), F32)...]
where the time goes in v3:
time: 29.3 us; the launch traced here: 29.1 us
  Pallas kernels  27.2 us (93%)
  local copies, waits for them, and re-layouts  1.25 us (4%)
  between operations  0.64 us (2%)
    pallas_call x1, Pallas kernels, body(): pl.pallas_call(kernel, out_shape=(jax.ShapeDtypeStruct((2, 16, 512), F32)...  27.2 us
    unnamed x2, local copies, waits for them, and re-layouts  1.25 us

profile of v3, /device:TPU:7, one launch (start us, length us, event | category | flops | bytes accessed | tf_op | source)
XLA Modules:
  0.0 29.1 jit_solution(1660032504052077504)
XLA Ops:
  0.6 27.2 %shard_map.104 = (f32[2,16,512]{2,1,0:T(8,128)S(1)}, bf16[2,16,512]{2,1,0:T(8,128)(2,1)S(1)}) custom-call(f32[2,512]{1,0:T(2,128)} %h0_hbm.1, f32[4,128]{1,0:T(4,128)} %bitcast.2, f32[2,16]{1,0:T(2,128)} %steps_hbm.1, f32[2,16,16]{2,1,0:T(8,128)} %inc_hbm.1, f32[16,4,128,128]{3,2,1,0:T(8,128)} %coup_hbm.1, f32[16,512]{1,0:T(8,128)} %iw_hbm.1, ...), custom_call_target="tpu_custom_call" | custom-call | flops 1000000000 | bytes 4000000 | tf_op jit(solution)/shard_map/pallas_call | solution.py:391
  27.9 0.6 %copy.13 = f32[2,16,512]{2,1,0:T(8,128)} copy(f32[2,16,512]{2,1,0:T(8,128)S(1)} %get-tuple-element.4) | data formatting | bytes 131072
  28.5 0.6 %copy.14 = bf16[2,16,512]{2,1,0:T(8,128)(2,1)} copy(bf16[2,16,512]{2,1,0:T(8,128)(2,1)S(1)} %get-tuple-element.5) | data formatting | bytes 65536

commit v4 on v3

--- a/solution.py
+++ b/solution.py
@@ -53,7 +53,7 @@
 def kernel(
     h0_hbm, decay_hbm, steps_hbm, inc_hbm, coup_hbm, iw_hbm, gain_hbm, vw_hbm, gw_hbm,
     states_ref, read_ref,
-    h0_ref, decay_ref, steps_ref, inc_ref, iw_ref, pack, incbuf, cbuf, vw, gw, gbuf, cth, ctl, xbuf, dc, sig, arow, prow, ns, na,
+    h0_ref, decay_ref, steps_ref, inc_ref, iw_ref, pack, incbuf, cbuf, vw, gw, gbuf, cth, xbuf, dc, sig, arow, prow, ns, na,
     dbuf, eb, tree, pref, msg, maps, starts, cols, stout, scout, stbuf, scbuf,
     local_sem, inc_ss, inc_rs, gain_ss, gain_rs, map_ss, map_rs, st_ss, st_rs,
 ):
@@ -133,17 +133,8 @@
     dc[0:L, :] = -to_column(decay_row)
     dc[L:ROWS, :] = jnp.zeros((ROWS - L, L), F32)
     load_c.wait()
-    for q in range(9):
-        if q == 8:
-            w = iw_ref[:, pl.ds(pl.multiple_of(lb * L, L), L)]
-            wide = jnp.broadcast_to(w[:, None, :], (16, 8, L))
-            first = jnp.where(iota((16, 8, L), 1) == 0, wide, 0.0).reshape(L, L)
-            second = jnp.zeros((L, L), F32)
-            for n, t in enumerate((first, second)):
-                hi, lo = split2(t)
-                cth[q, 0:L, n * L : (n + 1) * L] = hi
-                cth[q, L : 2 * L, n * L : (n + 1) * L] = hi
-                ctl[q, :, n * L : (n + 1) * L] = lo
+    drive = iw_ref[:, pl.ds(pl.multiple_of(lb * L, L), L)]
+    drive = jnp.concatenate([drive, jnp.zeros((L - 16, L), F32)], axis=0)
 
     def transpose_pair(cp, _):
         a = cbuf[2 * cp].T.reshape(16, 8, L)
@@ -155,7 +146,7 @@
             q, n = jb // 2, jb % 2
             cth[q, pl.ds(base, 16), n * L : (n + 1) * L] = hi[jb]
             cth[q, pl.ds(base + L, 16), n * L : (n + 1) * L] = hi[jb]
-            ctl[q, pl.ds(base, 16), n * L : (n + 1) * L] = lo[jb]
+            cth[q, pl.ds(base + 2 * L, 16), n * L : (n + 1) * L] = lo[jb]
         return 0
 
     lax.fori_loop(0, 8, transpose_pair, 0)
@@ -169,7 +160,10 @@
     for n, piece in enumerate(split2(incp)):
         wide = mm(piece, spread)
         x = jnp.where(keep, jnp.broadcast_to(wide[:, None, :], (L, 8, L)), 0.0)
-        xbuf[:, n * L : (n + 1) * L] = x.reshape(8 * L, L).astype(BF16)
+        x = x.reshape(8 * L, L).astype(BF16)
+        xbuf[:, n * L : (n + 1) * L] = x
+        if n == 0:
+            xbuf[:, 2 * L : 3 * L] = x
 
     stepbc = jnp.broadcast_to(incp[:, 16:17], (L, L))
     t_row, t_col = iota((L, L), 0), iota((L, L), 1)
@@ -199,9 +193,9 @@
         return dbuf[7 * 16 + i] if level == 0 else tree[first_of[level] - 16 + i]
 
     def build(q, m):
-        rows = 256
+        rows = 512
         x = xbuf[m * rows : (m + 1) * rows, :]
-        e = mm(x, cth[q]) + mm(x[:, :L], ctl[q])
+        e = mm(x, cth[q])
         nt = rows // 8
         t0, base = m * nt, q * 16
         s = sig[t0 : t0 + nt, :][:, None, :]
@@ -215,17 +209,23 @@
 
     def advance(t):
         d = dbuf[t - 16]
-        dbuf[t] = dbuf[t] + d * arow[t : t + 1, :] + mm(d.astype(BF16), eb[t, 0:L, :])
+        dbuf[t] = dbuf[t] + d * arow[t : t + 1, :] + mm(d.astype(BF16), eb[t])
+
+    inc_hi, inc_lo = split2(jnp.where(t_col < 16, incp, 0.0))
+    drive_hi, drive_lo = split2(drive)
+    vector = mm(inc_hi, drive_hi) + mm(inc_lo, drive_hi) + mm(inc_hi, drive_lo)
+    dbuf[:, L : L + 8, :] = jnp.where(iota((L, 8, L), 1) == 0, jnp.broadcast_to(vector[:, None, :], (L, 8, L)), 0.0)
+    dbuf[:, L + 8 : ROWS, :] = jnp.zeros((L, 8, L), F32)
 
     waiting = []
-    for m in range(4):
-        for q in range(9):
+    for m in range(2):
+        for q in range(8):
             build(q, m)
-            now = -(-len(waiting) // (9 - q))
+            now = -(-len(waiting) // (8 - q))
             for t in waiting[:now]:
                 advance(t)
             waiting = waiting[now:]
-        waiting = list(range(max(16, 32 * m), 32 * m + 32))
+        waiting = list(range(max(16, 64 * m), 64 * m + 64))
     for t in waiting:
         advance(t)
 
@@ -382,13 +382,21 @@
             copy.wait_send()
 
 
+def deliver(a_ref, b_ref, x_ref, y_ref, sem):
+    copies = [pltpu.make_async_copy(a_ref, x_ref, sem.at[0]), pltpu.make_async_copy(b_ref, y_ref, sem.at[1])]
+    for copy in copies:
+        copy.start()
+    for copy in copies:
+        copy.wait()
+
+
 def body(initial_state, decay_rate, step_sizes, increments, coupling, input_weight, gain, value_weight, gate_weight):
     args = (initial_state, decay_rate.reshape(4, L), step_sizes, increments, coupling, input_weight, gain.reshape(4, L),
             value_weight, gate_weight)
     args = [pltpu.with_memory_space_constraint(a, pltpu.HBM) for a in args]
     vmem, hbm = pl.BlockSpec(memory_space=pltpu.VMEM), pl.BlockSpec(memory_space=pltpu.HBM)
     dma = pltpu.SemaphoreType.DMA
-    return pl.pallas_call(
+    parts = pl.pallas_call(
         kernel,
         out_shape=(jax.ShapeDtypeStruct((2, 16, 512), F32), jax.ShapeDtypeStruct((2, 16, 512), BF16)),
         in_specs=[hbm] * 9,
@@ -405,9 +413,8 @@
             pltpu.VMEM((1024, 512), BF16),
             pltpu.VMEM((1024, 512), BF16),
             pltpu.VMEM((2, 4, L), F32),
-            pltpu.VMEM((9, 2 * L, 2 * L), BF16),
-            pltpu.VMEM((9, L, 2 * L), BF16),
-            pltpu.VMEM((8 * L, 2 * L), BF16),
+            pltpu.VMEM((8, 3 * L, 2 * L), BF16),
+            pltpu.VMEM((8 * L, 3 * L), BF16),
             pltpu.VMEM((ROWS, L), F32),
             pltpu.VMEM((L, L), F32),
             pltpu.VMEM((L, L), F32),
@@ -415,7 +422,7 @@
             pltpu.VMEM((NODES, L), F32),
             pltpu.VMEM((NODES, L), F32),
             pltpu.VMEM((L, ROWS, L), F32),
-            pltpu.VMEM((L, ROWS, L), BF16),
+            pltpu.VMEM((L, L, L), BF16),
             pltpu.VMEM((15, ROWS, L), F32),
             pltpu.VMEM((16, ROWS, L), F32),
             pltpu.VMEM((ROWS, L), BF16),
@@ -432,6 +439,15 @@
             collective_id=0, has_side_effects=True, vmem_limit_bytes=48 * 1024 * 1024),
         cost_estimate=pl.CostEstimate(flops=10**9, bytes_accessed=4 * 10**6, transcendentals=0),
     )(*args)
+    anywhere = pl.BlockSpec(memory_space=pl.ANY)
+    return pl.pallas_call(
+        deliver,
+        out_shape=(jax.ShapeDtypeStruct((2, 16, 512), F32), jax.ShapeDtypeStruct((2, 16, 512), BF16)),
+        in_specs=[anywhere] * 2,
+        out_specs=(hbm, hbm),
+        scratch_shapes=[dma((2,))],
+        compiler_params=pltpu.CompilerParams(vmem_limit_bytes=1024 * 1024),
+    )(*parts)
 
 
 def solution(mesh):

time: 29.3 us -> 28.6 us (0.976)
  local copies, waits for them, and re-layouts: 1.25 us -> 0 us
  Pallas kernels: 27.2 us -> 27.7 us
    unnamed x2 -> x0, local copies, waits for them, and re-layouts: 1.25 us -> none
    pallas_call x0 -> x1, Pallas kernels: none -> 0.66 us  [body(): pl.pallas_call(deliver, out_shape=(jax.ShapeDtypeStruct((2, 16, 512), F32...]
where the time goes in v4:
time: 28.6 us; the launch traced here: 28.4 us
  Pallas kernels  27.7 us (97%)
  between operations  0.64 us (2%)
    pallas_call x1, Pallas kernels, body(): pl.pallas_call(kernel, out_shape=(jax.ShapeDtypeStruct((2, 16, 512), F32)...  27.1 us
    pallas_call x1, Pallas kernels, body(): pl.pallas_call(deliver, out_shape=(jax.ShapeDtypeStruct((2, 16, 512), F32...  0.66 us

profile of v4, /device:TPU:7, one launch (start us, length us, event | category | flops | bytes accessed | tf_op | source)
XLA Modules:
  0.0 28.4 jit_solution(2843100095638702736)
XLA Ops:
  0.6 27.1 %shard_map.104 = (f32[2,16,512]{2,1,0:T(8,128)S(1)}, bf16[2,16,512]{2,1,0:T(8,128)(2,1)S(1)}) custom-call(f32[2,512]{1,0:T(2,128)} %h0_hbm.1, f32[4,128]{1,0:T(4,128)} %bitcast.2, f32[2,16]{1,0:T(2,128)} %steps_hbm.1, f32[2,16,16]{2,1,0:T(8,128)} %inc_hbm.1, f32[16,4,128,128]{3,2,1,0:T(8,128)} %coup_hbm.1, f32[16,512]{1,0:T(8,128)} %iw_hbm.1, ...), custom_call_target="tpu_custom_call" | custom-call | flops 1000000000 | bytes 4000000 | tf_op jit(solution)/shard_map/pallas_call | solution.py:399
  27.7 0.7 %shard_map.105 = (f32[2,16,512]{2,1,0:T(8,128)}, bf16[2,16,512]{2,1,0:T(8,128)(2,1)}) custom-call(f32[2,16,512]{2,1,0:T(8,128)S(1)} %get-tuple-element.4.a_ref, bf16[2,16,512]{2,1,0:T(8,128)(2,1)S(1)} %get-tuple-element.5.b_ref), custom_call_target="tpu_custom_call" | custom-call | tf_op jit(solution)/shard_map/pallas_call | solution.py:443

commit v5 on v4

--- a/solution.py
+++ b/solution.py
@@ -267,11 +267,11 @@
         def one(n, _):
             @pl.when(seg == 0)
             def _():
-                act(map_copy(seg, 7 - n, last))
+                act(map_copy(seg, seg + 1 + n, last))
 
             @pl.when(seg > 0)
             def _():
-                act(map_copy(seg, 7 - n, full))
+                act(map_copy(seg, seg + 1 + n, full))
 
             return 0
 

time: 28.6 us -> 28.2 us (0.986)
  Pallas kernels: 27.7 us -> 27.4 us
    pallas_call x1, Pallas kernels: 27.1 us -> 26.7 us  [body(): pl.pallas_call(kernel, out_shape=(jax.ShapeDtypeStruct((2, 16, 512), F32)...]
where the time goes in v5:
time: 28.2 us; the launch traced here: 28 us
  Pallas kernels  27.4 us (97%)
  between operations  0.64 us (2%)
    pallas_call x1, Pallas kernels, body(): pl.pallas_call(kernel, out_shape=(jax.ShapeDtypeStruct((2, 16, 512), F32)...  26.7 us
    pallas_call x1, Pallas kernels, body(): pl.pallas_call(deliver, out_shape=(jax.ShapeDtypeStruct((2, 16, 512), F32...  0.66 us

profile of v5, /device:TPU:7, one launch (start us, length us, event | category | flops | bytes accessed | tf_op | source)
XLA Modules:
  0.0 28.0 jit_solution(9903935429409837274)
XLA Ops:
  0.6 26.7 %shard_map.104 = (f32[2,16,512]{2,1,0:T(8,128)S(1)}, bf16[2,16,512]{2,1,0:T(8,128)(2,1)S(1)}) custom-call(f32[2,512]{1,0:T(2,128)} %h0_hbm.1, f32[4,128]{1,0:T(4,128)} %bitcast.2, f32[2,16]{1,0:T(2,128)} %steps_hbm.1, f32[2,16,16]{2,1,0:T(8,128)} %inc_hbm.1, f32[16,4,128,128]{3,2,1,0:T(8,128)} %coup_hbm.1, f32[16,512]{1,0:T(8,128)} %iw_hbm.1, ...), custom_call_target="tpu_custom_call" | custom-call | flops 1000000000 | bytes 4000000 | tf_op jit(solution)/shard_map/pallas_call | solution.py:399
  27.3 0.7 %shard_map.105 = (f32[2,16,512]{2,1,0:T(8,128)}, bf16[2,16,512]{2,1,0:T(8,128)(2,1)}) custom-call(f32[2,16,512]{2,1,0:T(8,128)S(1)} %get-tuple-element.4.a_ref, bf16[2,16,512]{2,1,0:T(8,128)(2,1)S(1)} %get-tuple-element.5.b_ref), custom_call_target="tpu_custom_call" | custom-call | tf_op jit(solution)/shard_map/pallas_call | solution.py:443
